TPU v7x, 32 devices: a whole 2x2x4 slice. The times are simulated.
32 devices in a mesh: parts: 2 (over y), blk: 4 (over z), reader: 4 (over x, core), sub: 1.
Axes of the slice: x: 2, y: 2, z: 4, core: 2. Of those that a mesh axis runs over, the one named last changes fastest.
Arguments:
- images: bfloat16 [3072, 8192], P(('parts', 'blk', 'reader'), 'sub'), parts along dimension 0, may hold values from -40 to 40
- routes: int32 [3072, 2], P(('parts', 'blk', 'reader')), parts along dimension 0, may hold values from 0 to 3, all different within a row; in each aligned block of 96 rows (0 to 95, 96 to 191, ...) at most 96 rows name the same one
- projections: bfloat16 [8, 128, 8192], P(('parts', 'reader'), 'blk', 'sub'), parts along dimension 0, may hold values from -8 to 8
- noise_weights: float32 [16384], P(('parts', 'sub')), parts along dimension 0, may hold values from 0.3 to 3
Outputs:
- weighted_sums: float32 [8, 128, 8192], P(('parts', 'reader'), 'blk', 'sub'), parts along dimension 0
- normalizer: float32 [3072], P(('parts', 'blk', 'reader')), parts along dimension 0
There are 2 independent parts, one for each index of `parts`. A program takes and returns all parts, laid end to end along the dimension named above; each array names one. Nothing has to cross between parts.
Inputs may be any that keep to these rules, and one draw needn't show every extreme that they name: `routes`: each row names 2 different class groups. In the rows of one device (aligned blocks of 96 rows) no group is named by more than 96 rows, a bound that some block reaches.
All inputs are finite; a program needn't handle non-finite values.
Results may differ from a plain program's by a relative error of at most 0.019.
Values may be sent and summed in bfloat16 or wider, within the bound.
A program may use at most 64 MiB of HBM per device.

v0:
```python
from functools import partial

import jax
import jax.numpy as jnp
from jax import lax
from jax.sharding import PartitionSpec as P


def from_behind(block, axis, distance):
    devices = range(lax.axis_size(axis))
    route = [((i - distance) % len(devices), i) for i in devices]
    return lax.ppermute(block, axis, route)


def slot_positions(route_block, groups):
    flat_routes = route_block.reshape(-1)
    onehot = (flat_routes[:, None] == jnp.arange(groups, dtype=jnp.int32)[None, :]).astype(
        jnp.int32
    )
    before = jnp.cumsum(onehot, axis=0) - onehot
    return jnp.sum(before * onehot, axis=1).reshape(route_block.shape)


def combine_stats(row_peaks, row_totals):
    highest = jnp.max(row_peaks, axis=-1)
    spread = row_totals * jnp.exp(row_peaks - highest[..., None])
    return highest + jnp.log(jnp.sum(spread, axis=-1))


def on_device(images, routes, projections, noise_weights):
    groups = lax.axis_size("reader")
    cycle_size = lax.axis_size("blk")
    my_group = lax.axis_index("reader")
    my_member = lax.axis_index("blk")
    per_device, top_count = routes.shape
    half_width = images.shape[1]
    capacity = min(per_device, 2 * per_device * top_count // groups)
    slot_count = groups * capacity
    ref_count = projections.shape[1]
    all_refs = ref_count * cycle_size
    anchor = jnp.zeros((), jnp.int32)
    own_index = slot_positions(routes, groups)
    own_target = routes * capacity + own_index
    sources = jnp.broadcast_to(jnp.arange(per_device, dtype=jnp.int32)[:, None], routes.shape)
    picker = (
        jnp.full((slot_count,), per_device, jnp.int32)
        .at[own_target.reshape(-1)]
        .set(sources.reshape(-1))
    )
    padded = jnp.concatenate([images, jnp.zeros((1, half_width), images.dtype)], axis=0)
    outgoing = padded[picker].reshape(groups, capacity, half_width)
    received = lax.all_to_all(outgoing, "reader", split_axis=0, concat_axis=0, tiled=True).reshape(
        slot_count, half_width
    )
    every_route = lax.all_gather(routes, "reader", axis=0, tiled=True).reshape(
        groups, per_device, top_count
    )
    every_index = jax.vmap(partial(slot_positions, groups=groups))(every_route)
    senders = jnp.arange(groups, dtype=jnp.int32)[:, None, None]
    landing = jnp.where(every_route == my_group, senders * capacity + every_index, slot_count)
    live_slot = jnp.zeros((slot_count,), jnp.int32).at[landing.reshape(-1)].set(1, mode="drop") > 0

    def score_block(ref_block):
        scaled = ref_block.astype(jnp.float32) * noise_weights[None, :]
        weighted = scaled.astype(jnp.bfloat16)
        penalty = 0.5 * jnp.sum(scaled * ref_block.astype(jnp.float32), axis=1)
        partial_scores = lax.dot_general(
            weighted, received, (((1,), (1,)), ((), ())), preferred_element_type=jnp.float32
        )
        partial_scores = partial_scores - penalty[:, None]
        return partial_scores

    def cycle_turn(rotation, carry):
        ref_block, score_table = carry
        position = (my_member - rotation) % cycle_size
        score_table = lax.dynamic_update_slice(
            score_table, score_block(ref_block)[None], (position, anchor, anchor)
        )
        ref_block = from_behind(ref_block, "blk", 1)
        return (ref_block, score_table)

    empty_table = jnp.zeros((cycle_size, ref_count, slot_count), jnp.float32)
    ref_block, score_table = lax.fori_loop(
        0, cycle_size - 1, cycle_turn, (projections[0], empty_table)
    )
    position = (my_member + 1) % cycle_size
    score_table = lax.dynamic_update_slice(
        score_table, score_block(ref_block)[None], (position, anchor, anchor)
    )
    score_table = lax.psum(score_table, "sub")
    scores = score_table.reshape(all_refs, slot_count)
    row_peak = jnp.max(scores, axis=0)
    row_total = jnp.sum(jnp.exp(scores - row_peak[None, :]), axis=0)
    back_peak, back_total = (
        lax.all_to_all(
            row_peak.reshape(groups, capacity), "reader", split_axis=0, concat_axis=0, tiled=True
        ),
        lax.all_to_all(
            row_total.reshape(groups, capacity), "reader", split_axis=0, concat_axis=0, tiled=True
        ),
    )
    normalizer = combine_stats(
        back_peak.reshape(-1)[own_target], back_total.reshape(-1)[own_target]
    )
    outgoing_norm = (
        jnp.zeros((slot_count,), jnp.float32)
        .at[own_target.reshape(-1)]
        .set(jnp.repeat(normalizer, top_count))
    )
    slot_norm = lax.all_to_all(
        outgoing_norm.reshape(groups, capacity), "reader", split_axis=0, concat_axis=0, tiled=True
    ).reshape(slot_count)
    exponent = jnp.where(live_slot[None, :], scores - slot_norm[None, :], -jnp.inf)
    posterior = jnp.exp(exponent).astype(jnp.bfloat16)
    summed = lax.psum_scatter(
        jnp.dot(posterior, received, preferred_element_type=jnp.float32).astype(jnp.bfloat16),
        "blk",
        scatter_dimension=0,
        tiled=True,
    ).astype(jnp.float32)
    return (summed[None], normalizer)


def solution(mesh):
    return jax.shard_map(
        on_device,
        mesh=mesh,
        in_specs=(
            P(("parts", "blk", "reader"), "sub"),
            P(("parts", "blk", "reader"), None),
            P(("parts", "reader"), "blk", "sub"),
            P(("parts", "sub")),
        ),
        out_specs=(P(("parts", "reader"), "blk", "sub"), P(("parts", "blk", "reader"))),
        check_vma=False,
    )
```

profile of v0, /device:TPU:20, one launch (start us, length us, event | category | flops | bytes accessed | tf_op | source)
XLA Modules:
  0.0 239.8 jit_solution(12317410076920263179)
XLA Ops:
  13.9 7.2 %gather_fusion = bf16[384,8192]{1,0:T(8,128)(2,1)} fusion(bf16[97,8192]{1,0:T(8,128)(2,1)S(1)} %concatenate.3, s32[1024]{0:T(1024)S(1)} %pad_clamp_fusion.1), kind=kCustom, calls=%fused_computation | custom fusion | bytes 12584448 | tf_op jit(solution)/shard_map/gather | solution.py:51
  21.1 5.4 %all-to-all-start = ((bf16[4,96,8192]{2,1,0:T(8,128)(2,1)}), bf16[4,96,8192]{2,1,0:T(8,128)(2,1)}, u32[]{:S(2)}, u32[]{:S(2)}) async-start(bf16[4,96,8192]{2,1,0:T(8,128)(2,1)} %bitcast.40), calls=%async_computation | async-start | bytes 12582912 | tf_op jit(solution)/shard_map/all_to_all | solution.py:52
  26.5 71.5 %all-gather = s32[4,96,2]{1,2,0:T(2,128)S(1)} all-gather(s32[1,96,2]{1,2,0:T(2,128)S(1)} %bitcast.45), channel_id=1, replica_groups=mesh['parts'=2,'blk'=4,'reader'=4,'sub'=1] {'reader'}, dimensions={0}, use_global_device_ids=true | all-gather | bytes 3840 | tf_op jit(solution)/shard_map/all_gather | solution.py:55
  98.3 4.8 %reduce-window.14 = s32[4,4,2,128]{3,2,1,0:T(2,128)S(1)} reduce-window(s32[4,4,2,128]{3,2,1,0:T(2,128)S(1)} %reshape.195, s32[]{:T(128)} %constant.106.clone.1), window={size=1x1x1x128 pad=0_0x0_0x0_0x127_0}, to_apply=%region_0.0 | reduce-window | flops 520192 | bytes 32772 | tf_op jit(solution)/shard_map/reduce-window
  104.3 40.2 %while.17 = (s32[]{:T(128)}, bf16[32,8192]{1,0:T(8,128)(2,1)S(1)}, f32[4,32,384]{2,1,0:T(8,128)S(1)}, f32[8192]{0:T(1024)S(1)}, bf16[384,8192]{1,0:T(8,128)(2,1)...) while((s32[]{:T(128)}, bf16[32,8192]{1,0:T(8,128)(2,1)S(1)}, ...), condition=%wide.region_10.11_spmd, body=%wide.region_8.10_spmd.sunk | while | flops 203173904 | bytes 10601644 | solution.py:83
  104.4 1.6 collective-permute-start
  106.3 4.8 %fusion.30 = f32[4,32,384]{2,1,0:T(8,128)S(1)} fusion(f32[4,32,384]{2,1,0:T(8,128)S(1)} %get-tuple-element.223, s32[]{:T(128)S(6)} %select_n.101, bf16[384,8192]{1,0:T(8,128)(2,1)} %get-tuple-element.235, bf16[32,8192]{1,0:T(8,128)(2,1)S(1)} %copy.54, f32[8192]{0:T(1024)S(1)} %get-tuple-element.234, f32[32]{0:T(128)S(1)} %broadcast_multiply_fusion.3), kind=kOutput, calls=%fused_computation.10.clone.1 | convolution fusion | flops 202125312 | bytes 6898180 | tf_op jit(solution)/shard_map/while/body/eval_jaxpr/dot_general | solution.py:67
  111.1 7.5 %collective-permute-done = bf16[32,8192]{1,0:T(8,128)(2,1)S(1)} collective-permute-done((bf16[32,8192]{1,0:T(8,128)(2,1)S(1)}, bf16[32,8192]{1,0:T(8,128)(2,1)S(1)}, u32[]{:S(2)}, u32[]{:S(2)}) %collective-permute-start) | collective-permute-done | bytes 524320 | tf_op jit(solution)/shard_map/while/body/eval_jaxpr/ppermute | solution.py:12
  118.6 1.6 collective-permute-start
  120.5 4.8 %fusion.30 = f32[4,32,384]{2,1,0:T(8,128)S(1)} fusion(f32[4,32,384]{2,1,0:T(8,128)S(1)} %get-tuple-element.223, s32[]{:T(128)S(6)} %select_n.101, bf16[384,8192]{1,0:T(8,128)(2,1)} %get-tuple-element.235, bf16[32,8192]{1,0:T(8,128)(2,1)S(1)} %copy.54, f32[8192]{0:T(1024)S(1)} %get-tuple-element.234, f32[32]{0:T(128)S(1)} %broadcast_multiply_fusion.3), kind=kOutput, calls=%fused_computation.10.clone.1 | convolution fusion | flops 202125312 | bytes 6898180 | tf_op jit(solution)/shard_map/while/body/eval_jaxpr/dot_general | solution.py:67
  125.3 6.7 %collective-permute-done = bf16[32,8192]{1,0:T(8,128)(2,1)S(1)} collective-permute-done((bf16[32,8192]{1,0:T(8,128)(2,1)S(1)}, bf16[32,8192]{1,0:T(8,128)(2,1)S(1)}, u32[]{:S(2)}, u32[]{:S(2)}) %collective-permute-start) | collective-permute-done | bytes 524320 | tf_op jit(solution)/shard_map/while/body/eval_jaxpr/ppermute | solution.py:12
  132.1 1.6 collective-permute-start
  134.0 4.8 %fusion.30 = f32[4,32,384]{2,1,0:T(8,128)S(1)} fusion(f32[4,32,384]{2,1,0:T(8,128)S(1)} %get-tuple-element.223, s32[]{:T(128)S(6)} %select_n.101, bf16[384,8192]{1,0:T(8,128)(2,1)} %get-tuple-element.235, bf16[32,8192]{1,0:T(8,128)(2,1)S(1)} %copy.54, f32[8192]{0:T(1024)S(1)} %get-tuple-element.234, f32[32]{0:T(128)S(1)} %broadcast_multiply_fusion.3), kind=kOutput, calls=%fused_computation.10.clone.1 | convolution fusion | flops 202125312 | bytes 6898180 | tf_op jit(solution)/shard_map/while/body/eval_jaxpr/dot_general | solution.py:67
  138.7 5.8 %collective-permute-done = bf16[32,8192]{1,0:T(8,128)(2,1)S(1)} collective-permute-done((bf16[32,8192]{1,0:T(8,128)(2,1)S(1)}, bf16[32,8192]{1,0:T(8,128)(2,1)S(1)}, u32[]{:S(2)}, u32[]{:S(2)}) %collective-permute-start) | collective-permute-done | bytes 524320 | tf_op jit(solution)/shard_map/while/body/eval_jaxpr/ppermute | solution.py:12
  144.8 4.8 %fusion.5 = f32[4,32,384]{2,1,0:T(8,128)S(1)} fusion(f32[4,32,384]{2,1,0:T(8,128)S(1)} %get-tuple-element.158, s32[]{:T(128)S(6)} %select_n.87, bf16[384,8192]{1,0:T(8,128)(2,1)} %bitcast.10, bf16[32,8192]{1,0:T(8,128)(2,1)S(1)} %get-tuple-element.159, f32[8192]{0:T(1024)S(1)} %get-tuple-element.248, f32[32]{0:T(128)S(1)} %broadcast_multiply_fusion.1), kind=kOutput, calls=%fused_computation.19 | convolution fusion | flops 202125312 | bytes 6898180 | tf_op jit(solution)/shard_map/dot_general | solution.py:67
  150.3 3.2 %all-to-all-start.2 = ((f32[4,1,96]{2,1,0:T(1,128)}), f32[4,1,96]{2,1,0:T(1,128)S(1)}, u32[]{:S(2)}, u32[]{:S(2)}) async-start(f32[4,1,96]{2,1,0:T(1,128)} %all_to_all.24), calls=%async_computation.2 | async-start | bytes 4096 | tf_op jit(solution)/shard_map/all_to_all | solution.py:98
  154.5 2.8 %all-to-all-done.2 = f32[4,1,96]{2,1,0:T(1,128)S(1)} async-done(((f32[4,1,96]{2,1,0:T(1,128)}), f32[4,1,96]{2,1,0:T(1,128)S(1)}, u32[]{:S(2)}, u32[]{:S(2)}) %all-to-all-start.2) | async-done | bytes 1568 | tf_op jit(solution)/shard_map/all_to_all | solution.py:98
  157.2 3.2 %all-to-all-start.1 = ((f32[4,1,96]{2,1,0:T(1,128)}), f32[4,1,96]{2,1,0:T(1,128)S(1)}, u32[]{:S(2)}, u32[]{:S(2)}) async-start(f32[4,1,96]{2,1,0:T(1,128)} %all_to_all.22), calls=%async_computation.1 | async-start | bytes 4096 | tf_op jit(solution)/shard_map/all_to_all | solution.py:95
  160.5 3.4 %scatter_custom_fusion = s32[384]{0:T(512)S(1)} fusion(s32[768]{0:T(1024)S(1)} %fusion.14, s32[768]{0:T(1024)S(1)} %broadcast.146, s32[]{:T(128)} %constant.106.clone.1), kind=kCustom, calls=%fused_computation.57 | custom fusion | bytes 1540 | tf_op jit(solution)/shard_map/scatter | solution.py:61
  171.7 3.2 %all-to-all-start.3 = ((f32[4,1,96]{2,1,0:T(1,128)}), f32[4,1,96]{2,1,0:T(1,128)S(1)}, u32[]{:S(2)}, u32[]{:S(2)}) async-start(f32[4,1,96]{2,1,0:T(1,128)} %all_to_all.26), calls=%async_computation.3 | async-start | bytes 4096 | tf_op jit(solution)/shard_map/all_to_all | solution.py:110
  175.0 3.6 %all-to-all-done.3 = f32[4,1,96]{2,1,0:T(1,128)S(1)} async-done(((f32[4,1,96]{2,1,0:T(1,128)}), f32[4,1,96]{2,1,0:T(1,128)S(1)}, u32[]{:S(2)}, u32[]{:S(2)}) %all-to-all-start.3) | async-done | bytes 1568 | tf_op jit(solution)/shard_map/all_to_all | solution.py:110
  179.3 5.4 %convolution_convert_fusion = bf16[128,8192]{1,0:T(8,128)(2,1)} fusion(bf16[128,384]{1,0:T(8,128)(2,1)S(1)} %bitcast.41, bf16[384,8192]{1,0:T(8,128)(2,1)} %bitcast.10), kind=kOutput, calls=%fused_computation.14 | convolution fusion | flops 806354944 | bytes 8486912 | tf_op jit(solution)/shard_map/dot_general | solution.py:116
  184.8 46.0 %reduce-scatter.2.cloned.1.call-done = bf16[32,8192]{1,0:T(8,128)(2,1)} async-done(((bf16[128,8192]{1,0:T(8,128)(2,1)}), bf16[32,8192]{1,0:T(8,128)(2,1)}) %reduce-scatter.2.cloned.1.call-update) | async-done | bytes 524304 | tf_op jit(solution)/shard_map/reduce_scatter | solution.py:115
  230.8 2.1 bitcast_convert_fusion
  (99 shorter events, 19.4 us)
Async XLA Ops:
  21.1 5.4 %copy-start.2 = (s32[96,2]{0,1:T(2,128)S(1)}, s32[96,2]{0,1:T(2,128)}, u32[]{:S(2)}) copy-start(s32[96,2]{0,1:T(2,128)} %param.7) | copy-start | bytes 2308
  21.1 83.3 %copy-start = (bf16[1,32,8192]{2,1,0:T(8,128)(2,1)S(1)}, bf16[1,32,8192]{2,1,0:T(8,128)(2,1)}, u32[]{:S(2)}) copy-start(bf16[1,32,8192]{2,1,0:T(8,128)(2,1)} %param.8) | copy-start | bytes 1572868
  21.1 83.3 %copy-start.1 = (f32[8192]{0:T(1024)S(1)}, f32[8192]{0:T(1024)}, u32[]{:S(2)}) copy-start(f32[8192]{0:T(1024)} %param.9) | copy-start | bytes 98308
  21.1 83.2 %all-to-all-start = ((bf16[4,96,8192]{2,1,0:T(8,128)(2,1)}), bf16[4,96,8192]{2,1,0:T(8,128)(2,1)}, u32[]{:S(2)}, u32[]{:S(2)}) async-start(bf16[4,96,8192]{2,1,0:T(8,128)(2,1)} %bitcast.40), calls=%async_computation | async-start | bytes 12582912 | tf_op jit(solution)/shard_map/all_to_all | solution.py:52
  104.4 14.2 %collective-permute-start = (bf16[32,8192]{1,0:T(8,128)(2,1)S(1)}, bf16[32,8192]{1,0:T(8,128)(2,1)S(1)}, u32[]{:S(2)}, u32[]{:S(2)}) collective-permute-start(bf16[32,8192]{1,0:T(8,128)(2,1)S(1)} %copy.54), channel_id=1, source_target_pairs={{12,0},{0,4},{4,8},{8,12},{13,1},{1,5},{5,9},{9,13},{14,2},{2,6},{... | collective-permute-start | bytes 1572872 | tf_op jit(solution)/shard_map/while/body/eval_jaxpr/ppermute | solution.py:12
  118.6 13.4 %collective-permute-start = (bf16[32,8192]{1,0:T(8,128)(2,1)S(1)}, bf16[32,8192]{1,0:T(8,128)(2,1)S(1)}, u32[]{:S(2)}, u32[]{:S(2)}) collective-permute-start(bf16[32,8192]{1,0:T(8,128)(2,1)S(1)} %copy.54), channel_id=1, source_target_pairs={{12,0},{0,4},{4,8},{8,12},{13,1},{1,5},{5,9},{9,13},{14,2},{2,6},{... | collective-permute-start | bytes 1572872 | tf_op jit(solution)/shard_map/while/body/eval_jaxpr/ppermute | solution.py:12
  132.1 12.5 %collective-permute-start = (bf16[32,8192]{1,0:T(8,128)(2,1)S(1)}, bf16[32,8192]{1,0:T(8,128)(2,1)S(1)}, u32[]{:S(2)}, u32[]{:S(2)}) collective-permute-start(bf16[32,8192]{1,0:T(8,128)(2,1)S(1)} %copy.54), channel_id=1, source_target_pairs={{12,0},{0,4},{4,8},{8,12},{13,1},{1,5},{5,9},{9,13},{14,2},{2,6},{... | collective-permute-start | bytes 1572872 | tf_op jit(solution)/shard_map/while/body/eval_jaxpr/ppermute | solution.py:12
  150.3 6.9 %all-to-all-start.2 = ((f32[4,1,96]{2,1,0:T(1,128)}), f32[4,1,96]{2,1,0:T(1,128)S(1)}, u32[]{:S(2)}, u32[]{:S(2)}) async-start(f32[4,1,96]{2,1,0:T(1,128)} %all_to_all.24), calls=%async_computation.2 | async-start | bytes 4096 | tf_op jit(solution)/shard_map/all_to_all | solution.py:98
  157.2 9.6 %all-to-all-start.1 = ((f32[4,1,96]{2,1,0:T(1,128)}), f32[4,1,96]{2,1,0:T(1,128)S(1)}, u32[]{:S(2)}, u32[]{:S(2)}) async-start(f32[4,1,96]{2,1,0:T(1,128)} %all_to_all.22), calls=%async_computation.1 | async-start | bytes 4096 | tf_op jit(solution)/shard_map/all_to_all | solution.py:95
  169.6 15.2 %copy-start.3 = (f32[96]{0:T(128)}, f32[96]{0:T(128)S(1)}, u32[]{:S(2)}) copy-start(f32[96]{0:T(128)S(1)} %log_add_fusion) | copy-start | bytes 1156
  171.7 6.9 %all-to-all-start.3 = ((f32[4,1,96]{2,1,0:T(1,128)}), f32[4,1,96]{2,1,0:T(1,128)S(1)}, u32[]{:S(2)}, u32[]{:S(2)}) async-start(f32[4,1,96]{2,1,0:T(1,128)} %all_to_all.26), calls=%async_computation.3 | async-start | bytes 4096 | tf_op jit(solution)/shard_map/all_to_all | solution.py:110
  174.9 55.9 %reduce-scatter.2.cloned.1.call-start = ((), (), s32[]{:S(2)}) async-start(), calls=%async_computation.5 | async-start | bytes 2621440 | tf_op jit(solution)/shard_map/reduce_scatter | solution.py:115
Sparse Core Ops, SparseCore 0:
  184.9 45.8 reduce-scatter.1
where the time goes:
time: 243 us; the launch traced here: 240 us
  waiting for transfers between devices  72.6 us (30%)
  blocking collectives  71.5 us (29%)
  local copies, waits for them, and re-layouts  24.4 us (10%)
  matrix products  24.4 us (10%)
  starting transfers between devices  19.9 us (8%)
  between operations  14.4 us (6%)
  other arithmetic  12.4 us (5%)
    all_gather x1, blocking collectives, on_device(): lax.all_gather(routes, 'reader', axis=0, tiled=True)  71.5 us
    reduce_scatter x1, waiting for transfers between devices, on_device(): lax.psum_scatter(jnp.dot(posterior, received, preferred_element_type=jnp....  46 us
    ppermute x3, waiting for transfers between devices, from_behind(): return lax.ppermute(block, axis, route)  20.1 us
    dot_general x4, matrix products, score_block(): lax.dot_general(weighted, received, (((1,), (1,)), ((), ())), preferred_e...  19 us
    gather x1, local copies, waits for them, and re-layouts, on_device(): outgoing = padded[picker].reshape(groups, capacity, half_width)  7.16 us
    another operation x7, other arithmetic  6.21 us
    dot_general x1, matrix products, on_device(): jnp.dot(posterior, received, preferred_element_type=jnp.float32)  5.44 us
    all_to_all x1, starting transfers between devices, on_device(): lax.all_to_all(outgoing, 'reader', split_axis=0, concat_axis=0, tiled=True)  5.38 us
  transfers between devices with their start and end apart: 8, of which 6 were waited for; matrix products, arithmetic and copies ran while one was open for 12% of the time, Pallas kernels for 0%

commit v1 on v0

--- a/solution.py
+++ b/solution.py
@@ -3,7 +3,11 @@
 import jax
 import jax.numpy as jnp
 from jax import lax
+from jax.experimental import pallas as pl
+from jax.experimental.pallas import tpu as pltpu
 from jax.sharding import PartitionSpec as P
+
+MESH = pl.DeviceIdType.MESH
 
 
 def from_behind(block, axis, distance):
@@ -12,13 +16,11 @@
     return lax.ppermute(block, axis, route)
 
 
-def slot_positions(route_block, groups):
-    flat_routes = route_block.reshape(-1)
-    onehot = (flat_routes[:, None] == jnp.arange(groups, dtype=jnp.int32)[None, :]).astype(
-        jnp.int32
-    )
-    before = jnp.cumsum(onehot, axis=0) - onehot
-    return jnp.sum(before * onehot, axis=1).reshape(route_block.shape)
+def slot_positions(route_block):
+    flat = route_block.reshape(-1)
+    order = jnp.arange(flat.shape[0], dtype=jnp.int32)
+    earlier = (order[None, :] < order[:, None]) & (flat[None, :] == flat[:, None])
+    return jnp.sum(earlier.astype(jnp.int32), axis=1).reshape(route_block.shape)
 
 
 def combine_stats(row_peaks, row_totals):
@@ -27,7 +29,7 @@
     return highest + jnp.log(jnp.sum(spread, axis=-1))
 
 
-def on_device(images, routes, projections, noise_weights):
+def routed(images, routes, projections, noise_weights):
     groups = lax.axis_size("reader")
     cycle_size = lax.axis_size("blk")
     my_group = lax.axis_index("reader")
@@ -39,7 +41,7 @@
     ref_count = projections.shape[1]
     all_refs = ref_count * cycle_size
     anchor = jnp.zeros((), jnp.int32)
-    own_index = slot_positions(routes, groups)
+    own_index = slot_positions(routes)
     own_target = routes * capacity + own_index
     sources = jnp.broadcast_to(jnp.arange(per_device, dtype=jnp.int32)[:, None], routes.shape)
     picker = (
@@ -55,7 +57,7 @@
     every_route = lax.all_gather(routes, "reader", axis=0, tiled=True).reshape(
         groups, per_device, top_count
     )
-    every_index = jax.vmap(partial(slot_positions, groups=groups))(every_route)
+    every_index = jax.vmap(slot_positions)(every_route)
     senders = jnp.arange(groups, dtype=jnp.int32)[:, None, None]
     landing = jnp.where(every_route == my_group, senders * capacity + every_index, slot_count)
     live_slot = jnp.zeros((slot_count,), jnp.int32).at[landing.reshape(-1)].set(1, mode="drop") > 0
@@ -67,8 +69,7 @@
         partial_scores = lax.dot_general(
             weighted, received, (((1,), (1,)), ((), ())), preferred_element_type=jnp.float32
         )
-        partial_scores = partial_scores - penalty[:, None]
-        return partial_scores
+        return partial_scores - penalty[:, None]
 
     def cycle_turn(rotation, carry):
         ref_block, score_table = carry
@@ -121,9 +122,382 @@
     return (summed[None], normalizer)
 
 
+def flipped(number, mask, size):
+    result, bit = 0, 1
+    while bit < size:
+        digit = lax.rem(lax.div(number, bit), 2)
+        result = result + bit * ((1 - digit) if mask & bit else digit)
+        bit *= 2
+    return result
+
+
+def kernel(
+    R, B,
+    images, routes, proj, noise,
+    out, norm,
+    X, PR, S, SR, Q, PART, UR, DR, US, DS, O,
+    loc, p_snd, p_rcv, x_snd, x_rcv, gu_snd, gd_snd, s_snd, s_rcv, q_snd, q_rcv,
+    u_snd, u_rcv, d_snd, d_rcv, o_snd, o_rcv,
+):
+    r = lax.axis_index("reader")
+    b = lax.axis_index("blk")
+    rows = images.shape[0]
+    refs = proj.shape[0]
+    Cs = X.shape[2]
+    width = R * refs
+    far = [k for k in range(R - 1, 1, -1)]
+    masks = far + [1]
+    peers = {k: flipped(r, k, R) for k in masks}
+    not_top = b < B - 1
+    not_bottom = b > 0
+
+    def span(i):
+        return pl.ds(pl.multiple_of(i * Cs, Cs), Cs)
+
+    def to_reader(src, dst, snd, rcv, k):
+        return pltpu.make_async_remote_copy(
+            src_ref=src, dst_ref=dst, send_sem=snd, recv_sem=rcv,
+            device_id={"reader": peers[k]}, device_id_type=MESH,
+        )
+
+    def to_blk(src, dst, snd, rcv, step):
+        return pltpu.make_async_remote_copy(
+            src_ref=src, dst_ref=dst, send_sem=snd, recv_sem=rcv,
+            device_id={"blk": b + step}, device_id_type=MESH,
+        )
+
+    def proj_copy(k):
+        return to_reader(proj.at[:, span(peers[k])], PR.at[b, r], p_snd.at[k], p_rcv.at[b, r], k)
+
+    def image_copy(k):
+        return to_reader(images.at[:, span(peers[k])], X.at[r], x_snd.at[k], x_rcv.at[r], k)
+
+    def gather_copy(src, g, step):
+        snd = gu_snd if step > 0 else gd_snd
+        return to_blk(PR.at[src, g], PR.at[src, g], snd.at[src, g], p_rcv.at[src, g], step)
+
+    def score_copy(src, k):
+        return to_reader(S.at[src, peers[k]], SR.at[src, r], s_snd.at[src, k], s_rcv.at[src, r], k)
+
+    def post_copy(k):
+        return to_reader(Q.at[:, r], Q.at[:, r], q_snd.at[k], q_rcv.at[r], k)
+
+    def up_copy(d, g):
+        return to_blk(US.at[d, g], UR.at[d, g], u_snd.at[d, g], u_rcv.at[d, g], 1)
+
+    def down_copy(d, g):
+        return to_blk(DS.at[d, g], DR.at[d, g], d_snd.at[d, g], d_rcv.at[d, g], -1)
+
+    def out_copy(k):
+        return to_reader(O.at[k], out.at[:, span(r)], o_snd.at[k], o_rcv.at[r], k)
+
+    def arrived(dst, sem):
+        to_reader(dst, dst, sem, sem, 1).wait_recv()
+
+    own_proj = pltpu.make_async_copy(proj.at[:, span(r)], PR.at[b, r], loc.at[0])
+    own_image = pltpu.make_async_copy(images.at[:, span(r)], X.at[r], loc.at[1])
+    own_proj.start()
+
+    barrier = pltpu.get_barrier_semaphore()
+    for k in masks:
+        pl.semaphore_signal(barrier, inc=1, device_id={"reader": peers[k]}, device_id_type=MESH)
+
+    @pl.when(not_top)
+    def _():
+        pl.semaphore_signal(barrier, inc=1, device_id={"blk": b + 1}, device_id_type=MESH)
+
+    @pl.when(not_bottom)
+    def _():
+        pl.semaphore_signal(barrier, inc=1, device_id={"blk": b - 1}, device_id_type=MESH)
+
+    pl.semaphore_wait(
+        barrier, (R - 1) + not_top.astype(jnp.int32) + not_bottom.astype(jnp.int32)
+    )
+
+    for k in masks:
+        proj_copy(k).start()
+    own_proj.wait()
+
+    def send_own(g):
+        @pl.when(not_top)
+        def _():
+            gather_copy(b, g, 1).start()
+
+        @pl.when(not_bottom)
+        def _():
+            gather_copy(b, g, -1).start()
+
+    send_own(r)
+    own_image.start()
+    for k in masks:
+        image_copy(k).start()
+    order = [1] + far[::-1]
+    for k in order:
+        arrived(PR.at[b, peers[k]], p_rcv.at[b, peers[k]])
+        send_own(peers[k])
+
+    tile = min(Cs, 512)
+
+    def score_chunk(src):
+        scores = jnp.zeros((R * rows, width), jnp.float32)
+        penalty = jnp.zeros((8, width), jnp.float32)
+        for t in range(Cs // tile):
+            cut = pl.ds(t * tile, tile)
+            refs_f = PR[src, :, :, cut].reshape(width, tile).astype(jnp.float32)
+            scaled = refs_f * noise[r, :, cut]
+            scores = scores + lax.dot_general(
+                X[:, :, cut].reshape(R * rows, tile), scaled.astype(jnp.bfloat16),
+                (((1,), (1,)), ((), ())), preferred_element_type=jnp.float32,
+            )
+            penalty = penalty + lax.dot_general(
+                jnp.full((8, tile), 0.5, jnp.float32), scaled * refs_f,
+                (((1,), (1,)), ((), ())), preferred_element_type=jnp.float32,
+                precision=lax.Precision.HIGHEST,
+            )
+        scores = scores - penalty[0:1]
+        S[src] = scores.reshape(R, rows, width)
+        for k in masks:
+            score_copy(src, k).start()
+
+    own_image.wait()
+    for k in order:
+        arrived(X.at[peers[k]], x_rcv.at[peers[k]])
+    score_chunk(b)
+
+    gather_order = [0] + order
+
+    def gather_step(dist, carry):
+        below, above = b - dist, b + dist
+        for k in gather_order:
+            g = flipped(r, k, R)
+
+            @pl.when(below >= 0)
+            def _():
+                arrived(PR.at[below, g], p_rcv.at[below, g])
+
+                @pl.when(not_top)
+                def _():
+                    gather_copy(below, g, 1).start()
+
+            @pl.when(above < B)
+            def _():
+                arrived(PR.at[above, g], p_rcv.at[above, g])
+
+                @pl.when(not_bottom)
+                def _():
+                    gather_copy(above, g, -1).start()
+
+        @pl.when(below >= 0)
+        def _():
+            score_chunk(below)
+
+        @pl.when(above < B)
+        def _():
+            score_chunk(above)
+
+        return carry
+
+    lax.fori_loop(1, B, gather_step, 0)
+
+    lane_group = lax.broadcasted_iota(jnp.int32, (rows, width), 1) // refs
+    named = (routes[:, 0:1] == lane_group) | (routes[:, 1:2] == lane_group)
+    chunks = []
+    for c in range(B):
+        total = S[c, r]
+        for k in masks:
+            arrived(SR.at[c, peers[k]], s_rcv.at[c, peers[k]])
+            total = total + SR[c, peers[k]]
+        chunks.append(jnp.where(named, total, -jnp.inf))
+    highest = chunks[0]
+    for c in range(1, B):
+        highest = jnp.maximum(highest, chunks[c])
+    highest = jnp.max(highest, axis=1, keepdims=True)
+    spread = jnp.exp(chunks[0] - highest)
+    for c in range(1, B):
+        spread = spread + jnp.exp(chunks[c] - highest)
+    normalizer = highest + jnp.log(jnp.sum(spread, axis=1, keepdims=True))
+    for c in range(B):
+        Q[c, r] = jnp.exp(chunks[c] - normalizer).astype(jnp.bfloat16)
+    for k in masks:
+        post_copy(k).start()
+    norm[...] = jnp.broadcast_to(normalizer, norm.shape)
+    for k in order:
+        arrived(Q.at[:, peers[k]], q_rcv.at[peers[k]])
+
+    def sum_chunk(d, dst):
+        posterior = Q[d].reshape(R * rows, width)
+        for t in range(Cs // tile):
+            cut = pl.ds(t * tile, tile)
+            product = lax.dot_general(
+                posterior, X[:, :, cut].reshape(R * rows, tile),
+                (((0,), (0,)), ((), ())), preferred_element_type=jnp.float32,
+            )
+            dst[d, :, :, cut] = product.reshape(R, refs, tile).astype(dst.dtype)
+
+    reduce_order = masks + [0]
+
+    def first_sums(step, carry):
+        up, down = B - 1 - step, step
+
+        @pl.when(b == 0)
+        def _():
+            sum_chunk(up, US)
+            for k in reduce_order:
+                up_copy(up, flipped(r, k, R)).start()
+
+        @pl.when(b == B - 1)
+        def _():
+            sum_chunk(down, DS)
+            for k in reduce_order:
+                down_copy(down, flipped(r, k, R)).start()
+
+        @pl.when((b > 0) & (up > b))
+        def _():
+            sum_chunk(up, PART)
+
+        @pl.when((b < B - 1) & (down < b))
+        def _():
+            sum_chunk(down, PART)
+
+        return carry
+
+    lax.fori_loop(0, B - 1, first_sums, 0)
+    sum_chunk(b, PART)
+
+    def pass_on(step, carry):
+        up, down = B - 1 - step, step
+        for k in reduce_order:
+            g = flipped(r, k, R)
+
+            @pl.when((b > 0) & (up > b))
+            def _():
+                arrived(UR.at[up, g], u_rcv.at[up, g])
+                US[up, g] = (PART[up, g] + UR[up, g].astype(jnp.float32)).astype(jnp.bfloat16)
+                up_copy(up, g).start()
+
+            @pl.when((b < B - 1) & (down < b))
+            def _():
+                arrived(DR.at[down, g], d_rcv.at[down, g])
+                DS[down, g] = (PART[down, g] + DR[down, g].astype(jnp.float32)).astype(jnp.bfloat16)
+                down_copy(down, g).start()
+
+        return carry
+
+    lax.fori_loop(0, B - 1, pass_on, 0)
+
+    own_out = pltpu.make_async_copy(O.at[0], out.at[:, span(r)], loc.at[0])
+    for k in reduce_order:
+        g = flipped(r, k, R)
+
+        @pl.when(not_bottom)
+        def _():
+            arrived(UR.at[b, g], u_rcv.at[b, g])
+            PART[b, g] = PART[b, g] + UR[b, g].astype(jnp.float32)
+
+        @pl.when(not_top)
+        def _():
+            arrived(DR.at[b, g], d_rcv.at[b, g])
+            PART[b, g] = PART[b, g] + DR[b, g].astype(jnp.float32)
+
+        O[k] = PART[b, g].astype(jnp.bfloat16)
+        if k:
+            out_copy(k).start()
+        else:
+            own_out.start()
+
+    for k in masks:
+        proj_copy(k).wait_send()
+        image_copy(k).wait_send()
+        post_copy(k).wait_send()
+
+    def sent(i, carry):
+        for k in masks:
+            score_copy(i, k).wait_send()
+        for g in range(R):
+            @pl.when(not_top & (i <= b))
+            def _():
+                gather_copy(i, g, 1).wait_send()
+
+            @pl.when(not_bottom & (i >= b))
+            def _():
+                gather_copy(i, g, -1).wait_send()
+
+            @pl.when(i > b)
+            def _():
+                up_copy(i, g).wait_send()
+
+            @pl.when(i < b)
+            def _():
+                down_copy(i, g).wait_send()
+
+        return carry
+
+    lax.fori_loop(0, B, sent, 0)
+    own_out.wait()
+    for k in masks:
+        out_copy(k).wait_send()
+        arrived(out.at[:, span(peers[k])], o_rcv.at[peers[k]])
+
+
+def split_coefficients(images, routes, projections, noise_weights):
+    R, B = lax.axis_size("reader"), lax.axis_size("blk")
+    rows, coef = images.shape
+    refs = projections.shape[1]
+    Cs, width = coef // R, R * refs
+    dma = pltpu.SemaphoreType.DMA
+    bf16, f32 = jnp.bfloat16, jnp.float32
+    sums, norm = pl.pallas_call(
+        partial(kernel, R, B),
+        out_shape=(
+            jax.ShapeDtypeStruct((refs, coef), bf16),
+            jax.ShapeDtypeStruct((rows, 128), f32),
+        ),
+        in_specs=[
+            pl.BlockSpec(memory_space=pl.ANY),
+            pl.BlockSpec(memory_space=pltpu.VMEM),
+            pl.BlockSpec(memory_space=pl.ANY),
+            pl.BlockSpec(memory_space=pltpu.VMEM),
+        ],
+        out_specs=(
+            pl.BlockSpec(memory_space=pl.ANY),
+            pl.BlockSpec(memory_space=pltpu.VMEM),
+        ),
+        scratch_shapes=[
+            pltpu.VMEM((R, rows, Cs), bf16),
+            pltpu.VMEM((B, R, refs, Cs), bf16),
+            pltpu.VMEM((B, R, rows, width), f32),
+            pltpu.VMEM((B, R, rows, width), f32),
+            pltpu.VMEM((B, R, rows, width), bf16),
+            pltpu.VMEM((B, R, refs, Cs), f32),
+            pltpu.VMEM((B, R, refs, Cs), bf16),
+            pltpu.VMEM((B, R, refs, Cs), bf16),
+            pltpu.VMEM((B, R, refs, Cs), bf16),
+            pltpu.VMEM((B, R, refs, Cs), bf16),
+            pltpu.VMEM((R, refs, Cs), bf16),
+            dma((2,)),
+            dma((R,)), dma((B, R)), dma((R,)), dma((R,)),
+            dma((B, R)), dma((B, R)),
+            dma((B, R)), dma((B, R)),
+            dma((R,)), dma((R,)),
+            dma((B, R)), dma((B, R)), dma((B, R)), dma((B, R)),
+            dma((R,)), dma((R,)),
+        ],
+        compiler_params=pltpu.CompilerParams(
+            collective_id=0, has_side_effects=True, vmem_limit_bytes=50 * 1024 * 1024
+        ),
+        cost_estimate=pl.CostEstimate(
+            flops=4 * R * rows * B * width * Cs, bytes_accessed=4 * rows * coef, transcendentals=0
+        ),
+    )(images, routes, projections[0], noise_weights.reshape(R, 1, Cs))
+    return (sums.astype(f32)[None], norm[:, 0])
+
+
 def solution(mesh):
+    sizes = dict(mesh.shape)
+    readers = sizes["reader"]
+    direct = sizes["sub"] == 1 and readers > 1 and readers & (readers - 1) == 0
     return jax.shard_map(
-        on_device,
+        split_coefficients if direct else routed,
         mesh=mesh,
         in_specs=(
             P(("parts", "blk", "reader"), "sub"),

time: 243 us -> 121 us (0.50); the launches traced: 240 us -> 121 us
  Pallas kernels: 0 us -> 115 us
  waiting for transfers between devices: 72.6 us -> 0 us
  blocking collectives: 71.5 us -> 0 us
  matrix products: 24.4 us -> 0 us
  starting transfers between devices: 19.9 us -> 0 us
  local copies, waits for them, and re-layouts: 24.4 us -> 4.6 us
  between operations: 14.4 us -> 0.65 us
  other arithmetic: 12.4 us -> 1.04 us
    pallas_call x0 -> x1, Pallas kernels: none -> 115 us  [split_coefficients(): pl.pallas_call(partial(kernel, R, B), out_shape=(jax.ShapeDtypeStruct((re...]
    all_gather x1 -> x0, blocking collectives: 71.5 us -> none  [on_device(): lax.all_gather(routes, 'reader', axis=0, tiled=True)]
    reduce_scatter x1 -> x0, waiting for transfers between devices: 46 us -> none  [on_device(): lax.psum_scatter(jnp.dot(posterior, received, preferred_element_type=jnp....]
    dot_general x5 -> x0, matrix products: 24.4 us -> none  [the longest x4 19 us: score_block(): lax.dot_general(weighted, received, (((1,), (1,)), ((), ())), preferred_e...]
    ppermute x3 -> x0, waiting for transfers between devices: 20.1 us -> none  [from_behind(): return lax.ppermute(block, axis, route)]
    all_to_all x4 -> x0, starting transfers between devices: 15 us -> none  [the longest x1 5.38 us: on_device(): lax.all_to_all(outgoing, 'reader', split_axis=0, concat_axis=0, tiled=True)]
    gather x5 -> x0, local copies, waits for them, and re-layouts: 10.6 us -> none  [the longest x1 7.16 us: on_device(): outgoing = padded[picker].reshape(groups, capacity, half_width)]
    all_to_all x4 -> x0, waiting for transfers between devices: 6.42 us -> none  [the longest x1 3.63 us: on_device(): lax.all_to_all(outgoing_norm.reshape(groups, capacity), 'reader', split_a...]
  transfers between devices with their start and end apart: 8 -> 0, of which waited for: 6 -> 0; matrix products, arithmetic and copies ran while one was open for 12% -> 0% of each run, Pallas kernels for 0% -> 0%
where the time goes in v1:
time: 121 us
  Pallas kernels  115 us (95%)
  local copies, waits for them, and re-layouts  4.6 us (4%)
    pallas_call x1, Pallas kernels, split_coefficients(): pl.pallas_call(partial(kernel, R, B), out_shape=(jax.ShapeDtypeStruct((re...  115 us
    unnamed x7, local copies, waits for them, and re-layouts  3.98 us

profile of v1, /device:TPU:20, one launch (start us, length us, event | category | flops | bytes accessed | tf_op | source)
XLA Modules:
  0.0 120.9 jit_solution(13575579943438574712)
XLA Ops:
  0.6 0.8 copy.7.routes
  1.4 0.0 copy-start
  1.4 1.4 %copy-done = bf16[96,8192]{1,0:T(8,128)(2,1)S(1)} copy-done((bf16[96,8192]{1,0:T(8,128)(2,1)S(1)}, bf16[96,8192]{1,0:T(8,128)(2,1)}, u32[]{:S(2)}) %copy-start) | copy-done | bytes 1572888
  2.8 0.0 copy-start.1
  2.8 1.0 copy-done.1
  3.9 0.0 copy-start.2
  3.9 0.8 copy-done.2
  4.6 114.6 %shard_map.59 = (bf16[32,8192]{1,0:T(8,128)(2,1)S(1)}, f32[96,128]{1,0:T(8,128)S(1)}) custom-call(bf16[96,8192]{1,0:T(8,128)(2,1)S(1)} %copy-done, s32[96,2]{1,0:T(8,128)S(1)} %copy.7.routes, bf16[32,8192]{1,0:T(8,128)(2,1)S(1)} %bitcast.5, f32[4,1,2048]{2,1,0:T(1,128)S(1)} %bitcast.6), custom_call_target="tpu_custom_call" | custom-call | flops 1610612736 | bytes 3145728 | tf_op jit(solution)/shard_map/pallas_call | solution.py:449
  119.2 0.6 slice_reduce_fusion
  119.8 1.0 bitcast_convert_fusion
Async XLA Ops:
  1.4 1.4 %copy-start = (bf16[96,8192]{1,0:T(8,128)(2,1)S(1)}, bf16[96,8192]{1,0:T(8,128)(2,1)}, u32[]{:S(2)}) copy-start(bf16[96,8192]{1,0:T(8,128)(2,1)} %images.1) | copy-start | bytes 4718596
  2.8 1.0 copy-start.1
  3.9 0.8 copy-start.2

commit v2 on v1

--- a/solution.py
+++ b/solution.py
@@ -144,6 +144,7 @@
     rows = images.shape[0]
     refs = proj.shape[0]
     Cs = X.shape[2]
+    T, tile = O.shape[0], O.shape[3]
     width = R * refs
     far = [k for k in range(R - 1, 1, -1)]
     masks = far + [1]
@@ -182,14 +183,20 @@
     def post_copy(k):
         return to_reader(Q.at[:, r], Q.at[:, r], q_snd.at[k], q_rcv.at[r], k)
 
-    def up_copy(d, g):
-        return to_blk(US.at[d, g], UR.at[d, g], u_snd.at[d, g], u_rcv.at[d, g], 1)
-
-    def down_copy(d, g):
-        return to_blk(DS.at[d, g], DR.at[d, g], d_snd.at[d, g], d_rcv.at[d, g], -1)
-
-    def out_copy(k):
-        return to_reader(O.at[k], out.at[:, span(r)], o_snd.at[k], o_rcv.at[r], k)
+    def up_copy(d, t):
+        return to_blk(US.at[d, t], UR.at[d, t], u_snd.at[d, t], u_rcv.at[d, t], 1)
+
+    def down_copy(d, t):
+        return to_blk(DS.at[d, t], DR.at[d, t], d_snd.at[d, t], d_rcv.at[d, t], -1)
+
+    def out_span(i, t):
+        return out.at[:, pl.ds(pl.multiple_of(i * Cs + t * tile, tile), tile)]
+
+    def out_copy(t, k):
+        return to_reader(O.at[t, peers[k]], out_span(r, t), o_snd.at[t, k], o_rcv.at[t, r], k)
+
+    def own_out(t):
+        return pltpu.make_async_copy(O.at[t, r], out_span(r, t), o_snd.at[t, 0])
 
     def arrived(dst, sem):
         to_reader(dst, dst, sem, sem, 1).wait_recv()
@@ -235,8 +242,6 @@
     for k in order:
         arrived(PR.at[b, peers[k]], p_rcv.at[b, peers[k]])
         send_own(peers[k])
-
-    tile = min(Cs, 512)
 
     def score_chunk(src):
         scores = jnp.zeros((R * rows, width), jnp.float32)
@@ -259,45 +264,50 @@
         for k in masks:
             score_copy(src, k).start()
 
+    gather_order = [0] + order
+
+    def forward(dist, carry):
+        below, above = b - dist, b + dist
+        for k in gather_order:
+            g = flipped(r, k, R)
+
+            @pl.when(below >= 0)
+            def _():
+                arrived(PR.at[below, g], p_rcv.at[below, g])
+
+                @pl.when(not_top)
+                def _():
+                    gather_copy(below, g, 1).start()
+
+            @pl.when(above < B)
+            def _():
+                arrived(PR.at[above, g], p_rcv.at[above, g])
+
+                @pl.when(not_bottom)
+                def _():
+                    gather_copy(above, g, -1).start()
+
+        return carry
+
+    def score_pair(dist, carry):
+        @pl.when(b - dist >= 0)
+        def _():
+            score_chunk(b - dist)
+
+        @pl.when(b + dist < B)
+        def _():
+            score_chunk(b + dist)
+
+        return carry
+
+    lax.fori_loop(1, B - 1, forward, 0)
     own_image.wait()
     for k in order:
         arrived(X.at[peers[k]], x_rcv.at[peers[k]])
     score_chunk(b)
-
-    gather_order = [0] + order
-
-    def gather_step(dist, carry):
-        below, above = b - dist, b + dist
-        for k in gather_order:
-            g = flipped(r, k, R)
-
-            @pl.when(below >= 0)
-            def _():
-                arrived(PR.at[below, g], p_rcv.at[below, g])
-
-                @pl.when(not_top)
-                def _():
-                    gather_copy(below, g, 1).start()
-
-            @pl.when(above < B)
-            def _():
-                arrived(PR.at[above, g], p_rcv.at[above, g])
-
-                @pl.when(not_bottom)
-                def _():
-                    gather_copy(above, g, -1).start()
-
-        @pl.when(below >= 0)
-        def _():
-            score_chunk(below)
-
-        @pl.when(above < B)
-        def _():
-            score_chunk(above)
-
-        return carry
-
-    lax.fori_loop(1, B, gather_step, 0)
+    lax.fori_loop(1, B - 1, score_pair, 0)
+    forward(B - 1, 0)
+    score_pair(B - 1, 0)
 
     lane_group = lax.broadcasted_iota(jnp.int32, (rows, width), 1) // refs
     named = (routes[:, 0:1] == lane_group) | (routes[:, 1:2] == lane_group)
@@ -324,86 +334,60 @@
     for k in order:
         arrived(Q.at[:, peers[k]], q_rcv.at[peers[k]])
 
-    def sum_chunk(d, dst):
-        posterior = Q[d].reshape(R * rows, width)
-        for t in range(Cs // tile):
-            cut = pl.ds(t * tile, tile)
-            product = lax.dot_general(
-                posterior, X[:, :, cut].reshape(R * rows, tile),
-                (((0,), (0,)), ((), ())), preferred_element_type=jnp.float32,
-            )
-            dst[d, :, :, cut] = product.reshape(R, refs, tile).astype(dst.dtype)
-
-    reduce_order = masks + [0]
-
-    def first_sums(step, carry):
+    def product(d, t):
+        return lax.dot_general(
+            Q[d].reshape(R * rows, width), X[:, :, pl.ds(t * tile, tile)].reshape(R * rows, tile),
+            (((0,), (0,)), ((), ())), preferred_element_type=jnp.float32,
+        )
+
+    def reduce_step(step, carry):
         up, down = B - 1 - step, step
-
-        @pl.when(b == 0)
-        def _():
-            sum_chunk(up, US)
-            for k in reduce_order:
-                up_copy(up, flipped(r, k, R)).start()
-
-        @pl.when(b == B - 1)
-        def _():
-            sum_chunk(down, DS)
-            for k in reduce_order:
-                down_copy(down, flipped(r, k, R)).start()
-
-        @pl.when((b > 0) & (up > b))
-        def _():
-            sum_chunk(up, PART)
-
-        @pl.when((b < B - 1) & (down < b))
-        def _():
-            sum_chunk(down, PART)
+        for t in range(T):
+            @pl.when(b == 0)
+            def _():
+                US[up, t] = product(up, t).astype(jnp.bfloat16)
+                up_copy(up, t).start()
+
+            @pl.when(b == B - 1)
+            def _():
+                DS[down, t] = product(down, t).astype(jnp.bfloat16)
+                down_copy(down, t).start()
+
+            @pl.when((b > 0) & (up > b))
+            def _():
+                own = product(up, t)
+                arrived(UR.at[up, t], u_rcv.at[up, t])
+                US[up, t] = (own + UR[up, t].astype(jnp.float32)).astype(jnp.bfloat16)
+                up_copy(up, t).start()
+
+            @pl.when((b < B - 1) & (down < b))
+            def _():
+                own = product(down, t)
+                arrived(DR.at[down, t], d_rcv.at[down, t])
+                DS[down, t] = (own + DR[down, t].astype(jnp.float32)).astype(jnp.bfloat16)
+                down_copy(down, t).start()
 
         return carry
 
-    lax.fori_loop(0, B - 1, first_sums, 0)
-    sum_chunk(b, PART)
-
-    def pass_on(step, carry):
-        up, down = B - 1 - step, step
-        for k in reduce_order:
-            g = flipped(r, k, R)
-
-            @pl.when((b > 0) & (up > b))
-            def _():
-                arrived(UR.at[up, g], u_rcv.at[up, g])
-                US[up, g] = (PART[up, g] + UR[up, g].astype(jnp.float32)).astype(jnp.bfloat16)
-                up_copy(up, g).start()
-
-            @pl.when((b < B - 1) & (down < b))
-            def _():
-                arrived(DR.at[down, g], d_rcv.at[down, g])
-                DS[down, g] = (PART[down, g] + DR[down, g].astype(jnp.float32)).astype(jnp.bfloat16)
-                down_copy(down, g).start()
-
-        return carry
-
-    lax.fori_loop(0, B - 1, pass_on, 0)
-
-    own_out = pltpu.make_async_copy(O.at[0], out.at[:, span(r)], loc.at[0])
-    for k in reduce_order:
-        g = flipped(r, k, R)
-
+    lax.fori_loop(0, B - 1, reduce_step, 0)
+
+    for t in range(T):
+        PART[t] = product(b, t)
+    for t in range(T):
         @pl.when(not_bottom)
         def _():
-            arrived(UR.at[b, g], u_rcv.at[b, g])
-            PART[b, g] = PART[b, g] + UR[b, g].astype(jnp.float32)
+            arrived(UR.at[b, t], u_rcv.at[b, t])
+            PART[t] = PART[t] + UR[b, t].astype(jnp.float32)
 
         @pl.when(not_top)
         def _():
-            arrived(DR.at[b, g], d_rcv.at[b, g])
-            PART[b, g] = PART[b, g] + DR[b, g].astype(jnp.float32)
-
-        O[k] = PART[b, g].astype(jnp.bfloat16)
-        if k:
-            out_copy(k).start()
-        else:
-            own_out.start()
+            arrived(DR.at[b, t], d_rcv.at[b, t])
+            PART[t] = PART[t] + DR[b, t].astype(jnp.float32)
+
+        O[t] = PART[t].reshape(R, refs, tile).astype(jnp.bfloat16)
+        for k in masks:
+            out_copy(t, k).start()
+        own_out(t).start()
 
     for k in masks:
         proj_copy(k).wait_send()
@@ -422,21 +406,23 @@
             def _():
                 gather_copy(i, g, -1).wait_send()
 
+        for t in range(T):
             @pl.when(i > b)
             def _():
-                up_copy(i, g).wait_send()
+                up_copy(i, t).wait_send()
 
             @pl.when(i < b)
             def _():
-                down_copy(i, g).wait_send()
+                down_copy(i, t).wait_send()
 
         return carry
 
     lax.fori_loop(0, B, sent, 0)
-    own_out.wait()
-    for k in masks:
-        out_copy(k).wait_send()
-        arrived(out.at[:, span(peers[k])], o_rcv.at[peers[k]])
+    for t in range(T):
+        own_out(t).wait()
+        for k in masks:
+            out_copy(t, k).wait_send()
+            arrived(out_span(peers[k], t), o_rcv.at[t, peers[k]])
 
 
 def split_coefficients(images, routes, projections, noise_weights):
@@ -444,6 +430,8 @@
     rows, coef = images.shape
     refs = projections.shape[1]
     Cs, width = coef // R, R * refs
+    tile = min(Cs, 512)
+    T = Cs // tile
     dma = pltpu.SemaphoreType.DMA
     bf16, f32 = jnp.bfloat16, jnp.float32
     sums, norm = pl.pallas_call(
@@ -468,19 +456,19 @@
             pltpu.VMEM((B, R, rows, width), f32),
             pltpu.VMEM((B, R, rows, width), f32),
             pltpu.VMEM((B, R, rows, width), bf16),
-            pltpu.VMEM((B, R, refs, Cs), f32),
-            pltpu.VMEM((B, R, refs, Cs), bf16),
-            pltpu.VMEM((B, R, refs, Cs), bf16),
-            pltpu.VMEM((B, R, refs, Cs), bf16),
-            pltpu.VMEM((B, R, refs, Cs), bf16),
-            pltpu.VMEM((R, refs, Cs), bf16),
+            pltpu.VMEM((T, width, tile), f32),
+            pltpu.VMEM((B, T, width, tile), bf16),
+            pltpu.VMEM((B, T, width, tile), bf16),
+            pltpu.VMEM((B, T, width, tile), bf16),
+            pltpu.VMEM((B, T, width, tile), bf16),
+            pltpu.VMEM((T, R, refs, tile), bf16),
             dma((2,)),
             dma((R,)), dma((B, R)), dma((R,)), dma((R,)),
             dma((B, R)), dma((B, R)),
             dma((B, R)), dma((B, R)),
             dma((R,)), dma((R,)),
-            dma((B, R)), dma((B, R)), dma((B, R)), dma((B, R)),
-            dma((R,)), dma((R,)),
+            dma((B, T)), dma((B, T)), dma((B, T)), dma((B, T)),
+            dma((T, R)), dma((T, R)),
         ],
         compiler_params=pltpu.CompilerParams(
             collective_id=0, has_side_effects=True, vmem_limit_bytes=50 * 1024 * 1024

time: 121 us -> 112 us (0.926)
  Pallas kernels: 115 us -> 106 us
    pallas_call x1, Pallas kernels: 115 us -> 106 us  [split_coefficients(): pl.pallas_call(partial(kernel, R, B), out_shape=(jax.ShapeDtypeStruct((re...]
where the time goes in v2:
time: 112 us
  Pallas kernels  106 us (95%)
  local copies, waits for them, and re-layouts  4.6 us (4%)
    pallas_call x1, Pallas kernels, split_coefficients(): pl.pallas_call(partial(kernel, R, B), out_shape=(jax.ShapeDtypeStruct((re...  106 us
    unnamed x7, local copies, waits for them, and re-layouts  3.98 us

profile of v2, /device:TPU:20, one launch (start us, length us, event | category | flops | bytes accessed | tf_op | source)
XLA Modules:
  0.0 112.0 jit_solution(2672676612636378207)
XLA Ops:
  0.6 0.8 copy.7.routes
  1.4 0.0 copy-start
  1.4 1.4 %copy-done = bf16[96,8192]{1,0:T(8,128)(2,1)S(1)} copy-done((bf16[96,8192]{1,0:T(8,128)(2,1)S(1)}, bf16[96,8192]{1,0:T(8,128)(2,1)}, u32[]{:S(2)}) %copy-start) | copy-done | bytes 1572888
  2.8 0.0 copy-start.1
  2.8 1.0 copy-done.1
  3.9 0.0 copy-start.2
  3.9 0.8 copy-done.2
  4.6 105.7 %shard_map.59 = (bf16[32,8192]{1,0:T(8,128)(2,1)S(1)}, f32[96,128]{1,0:T(8,128)S(1)}) custom-call(bf16[96,8192]{1,0:T(8,128)(2,1)S(1)} %copy-done, s32[96,2]{1,0:T(8,128)S(1)} %copy.7.routes, bf16[32,8192]{1,0:T(8,128)(2,1)S(1)} %bitcast.5, f32[4,1,2048]{2,1,0:T(1,128)S(1)} %bitcast.6), custom_call_target="tpu_custom_call" | custom-call | flops 1610612736 | bytes 3145728 | tf_op jit(solution)/shard_map/pallas_call | solution.py:437
  110.3 0.6 slice_reduce_fusion
  111.0 1.0 bitcast_convert_fusion
Async XLA Ops:
  1.4 1.4 %copy-start = (bf16[96,8192]{1,0:T(8,128)(2,1)S(1)}, bf16[96,8192]{1,0:T(8,128)(2,1)}, u32[]{:S(2)}) copy-start(bf16[96,8192]{1,0:T(8,128)(2,1)} %images.1) | copy-start | bytes 4718596
  2.8 1.0 copy-start.1
  3.9 0.8 copy-start.2

commit v3 on v2

--- a/solution.py
+++ b/solution.py
@@ -133,8 +133,9 @@
 
 def kernel(
     R, B,
-    images, routes, proj, noise,
+    images, routes_in, proj, noise_in,
     out, norm,
+    routes, noise,
     X, PR, S, SR, Q, PART, UR, DR, US, DS, O,
     loc, p_snd, p_rcv, x_snd, x_rcv, gu_snd, gd_snd, s_snd, s_rcv, q_snd, q_rcv,
     u_snd, u_rcv, d_snd, d_rcv, o_snd, o_rcv,
@@ -148,6 +149,7 @@
     width = R * refs
     far = [k for k in range(R - 1, 1, -1)]
     masks = far + [1]
+    order = [1] + far[::-1]
     peers = {k: flipped(r, k, R) for k in masks}
     not_top = b < B - 1
     not_bottom = b > 0
@@ -180,8 +182,8 @@
     def score_copy(src, k):
         return to_reader(S.at[src, peers[k]], SR.at[src, r], s_snd.at[src, k], s_rcv.at[src, r], k)
 
-    def post_copy(k):
-        return to_reader(Q.at[:, r], Q.at[:, r], q_snd.at[k], q_rcv.at[r], k)
+    def post_copy(c, k):
+        return to_reader(Q.at[c, r], Q.at[c, r], q_snd.at[c, k], q_rcv.at[c, r], k)
 
     def up_copy(d, t):
         return to_blk(US.at[d, t], UR.at[d, t], u_snd.at[d, t], u_rcv.at[d, t], 1)
@@ -204,6 +206,10 @@
     own_proj = pltpu.make_async_copy(proj.at[:, span(r)], PR.at[b, r], loc.at[0])
     own_image = pltpu.make_async_copy(images.at[:, span(r)], X.at[r], loc.at[1])
     own_proj.start()
+    noise_copy = pltpu.make_async_copy(noise_in, noise, loc.at[2])
+    noise_copy.start()
+    routes_copy = pltpu.make_async_copy(routes_in, routes, loc.at[3])
+    routes_copy.start()
 
     barrier = pltpu.get_barrier_semaphore()
     for k in masks:
@@ -221,7 +227,7 @@
         barrier, (R - 1) + not_top.astype(jnp.int32) + not_bottom.astype(jnp.int32)
     )
 
-    for k in masks:
+    for k in order:
         proj_copy(k).start()
     own_proj.wait()
 
@@ -238,28 +244,31 @@
     own_image.start()
     for k in masks:
         image_copy(k).start()
-    order = [1] + far[::-1]
     for k in order:
         arrived(PR.at[b, peers[k]], p_rcv.at[b, peers[k]])
         send_own(peers[k])
 
     def score_chunk(src):
         scores = jnp.zeros((R * rows, width), jnp.float32)
-        penalty = jnp.zeros((8, width), jnp.float32)
+        penalty = jnp.zeros((width, 128), jnp.float32)
         for t in range(Cs // tile):
             cut = pl.ds(t * tile, tile)
             refs_f = PR[src, :, :, cut].reshape(width, tile).astype(jnp.float32)
-            scaled = refs_f * noise[r, :, cut]
+            weights = noise[pl.ds(pl.multiple_of(r * Cs + t * tile, tile), tile)]
+            scaled = refs_f * weights[None, :]
             scores = scores + lax.dot_general(
                 X[:, :, cut].reshape(R * rows, tile), scaled.astype(jnp.bfloat16),
                 (((1,), (1,)), ((), ())), preferred_element_type=jnp.float32,
             )
-            penalty = penalty + lax.dot_general(
-                jnp.full((8, tile), 0.5, jnp.float32), scaled * refs_f,
-                (((1,), (1,)), ((), ())), preferred_element_type=jnp.float32,
-                precision=lax.Precision.HIGHEST,
-            )
-        scores = scores - penalty[0:1]
+            squares = scaled * refs_f
+            for lane in range(0, tile, 128):
+                penalty = penalty + squares[:, lane : lane + 128]
+        penalty_row = lax.dot_general(
+            jnp.full((8, 128), 0.5, jnp.float32), penalty,
+            (((1,), (1,)), ((), ())), preferred_element_type=jnp.float32,
+            precision=lax.Precision.HIGHEST,
+        )
+        scores = scores - penalty_row[0:1]
         S[src] = scores.reshape(R, rows, width)
         for k in masks:
             score_copy(src, k).start()
@@ -301,6 +310,8 @@
         return carry
 
     lax.fori_loop(1, B - 1, forward, 0)
+    noise_copy.wait()
+    routes_copy.wait()
     own_image.wait()
     for k in order:
         arrived(X.at[peers[k]], x_rcv.at[peers[k]])
@@ -310,7 +321,15 @@
     score_pair(B - 1, 0)
 
     lane_group = lax.broadcasted_iota(jnp.int32, (rows, width), 1) // refs
-    named = (routes[:, 0:1] == lane_group) | (routes[:, 1:2] == lane_group)
+    diagonal = lax.broadcasted_iota(jnp.int32, (rows, rows), 0) == lax.broadcasted_iota(
+        jnp.int32, (rows, rows), 1
+    )
+
+    def column(row):
+        return jnp.sum(jnp.where(diagonal, row, 0.0), axis=1, keepdims=True).astype(jnp.int32)
+
+    names = routes[...].astype(jnp.float32)
+    named = (column(names[0:1]) == lane_group) | (column(names[1:2]) == lane_group)
     chunks = []
     for c in range(B):
         total = S[c, r]
@@ -326,51 +345,74 @@
     for c in range(1, B):
         spread = spread + jnp.exp(chunks[c] - highest)
     normalizer = highest + jnp.log(jnp.sum(spread, axis=1, keepdims=True))
-    for c in range(B):
+    for c in sorted(range(B), key=lambda c: min(c, B - 1 - c)):
         Q[c, r] = jnp.exp(chunks[c] - normalizer).astype(jnp.bfloat16)
-    for k in masks:
-        post_copy(k).start()
+        for k in masks:
+            post_copy(c, k).start()
     norm[...] = jnp.broadcast_to(normalizer, norm.shape)
-    for k in order:
-        arrived(Q.at[:, peers[k]], q_rcv.at[peers[k]])
-
     def product(d, t):
+        cut = pl.ds(pl.multiple_of(t * tile, tile), tile)
         return lax.dot_general(
-            Q[d].reshape(R * rows, width), X[:, :, pl.ds(t * tile, tile)].reshape(R * rows, tile),
+            Q[d].reshape(R * rows, width), X[:, :, cut].reshape(R * rows, tile),
             (((0,), (0,)), ((), ())), preferred_element_type=jnp.float32,
         )
 
-    def reduce_step(step, carry):
-        up, down = B - 1 - step, step
-        for t in range(T):
+    def whole(d):
+        for k in order:
+            arrived(Q.at[d, peers[k]], q_rcv.at[d, peers[k]])
+
+    pieces = (B - 1) * T
+
+    def reduce_step(turn, carry):
+        n = turn - b
+        up, t = B - 1 - n // T, n % T
+
+        @pl.when((n >= 0) & (n < pieces) & (up > b))
+        def _():
+            @pl.when(t == 0)
+            def _():
+                whole(up)
+
+            own = product(up, t)
+
             @pl.when(b == 0)
             def _():
-                US[up, t] = product(up, t).astype(jnp.bfloat16)
-                up_copy(up, t).start()
-
-            @pl.when(b == B - 1)
-            def _():
-                DS[down, t] = product(down, t).astype(jnp.bfloat16)
-                down_copy(down, t).start()
-
-            @pl.when((b > 0) & (up > b))
-            def _():
-                own = product(up, t)
+                US[up, t] = own.astype(jnp.bfloat16)
+
+            @pl.when(b > 0)
+            def _():
                 arrived(UR.at[up, t], u_rcv.at[up, t])
                 US[up, t] = (own + UR[up, t].astype(jnp.float32)).astype(jnp.bfloat16)
-                up_copy(up, t).start()
-
-            @pl.when((b < B - 1) & (down < b))
-            def _():
-                own = product(down, t)
-                arrived(DR.at[down, t], d_rcv.at[down, t])
-                DS[down, t] = (own + DR[down, t].astype(jnp.float32)).astype(jnp.bfloat16)
-                down_copy(down, t).start()
+
+            up_copy(up, t).start()
+
+        m = turn - (B - 1 - b)
+        down, s = m // T, m % T
+
+        @pl.when((m >= 0) & (m < pieces) & (down < b))
+        def _():
+            @pl.when(s == 0)
+            def _():
+                whole(down)
+
+            own = product(down, s)
+
+            @pl.when(b == B - 1)
+            def _():
+                DS[down, s] = own.astype(jnp.bfloat16)
+
+            @pl.when(b < B - 1)
+            def _():
+                arrived(DR.at[down, s], d_rcv.at[down, s])
+                DS[down, s] = (own + DR[down, s].astype(jnp.float32)).astype(jnp.bfloat16)
+
+            down_copy(down, s).start()
 
         return carry
 
-    lax.fori_loop(0, B - 1, reduce_step, 0)
-
+    lax.fori_loop(0, pieces + B - 1, reduce_step, 0)
+
+    whole(b)
     for t in range(T):
         PART[t] = product(b, t)
     for t in range(T):
@@ -392,11 +434,11 @@
     for k in masks:
         proj_copy(k).wait_send()
         image_copy(k).wait_send()
-        post_copy(k).wait_send()
 
     def sent(i, carry):
         for k in masks:
             score_copy(i, k).wait_send()
+            post_copy(i, k).wait_send()
         for g in range(R):
             @pl.when(not_top & (i <= b))
             def _():
@@ -441,16 +483,18 @@
             jax.ShapeDtypeStruct((rows, 128), f32),
         ),
         in_specs=[
-            pl.BlockSpec(memory_space=pl.ANY),
-            pl.BlockSpec(memory_space=pltpu.VMEM),
-            pl.BlockSpec(memory_space=pl.ANY),
-            pl.BlockSpec(memory_space=pltpu.VMEM),
+            pl.BlockSpec(memory_space=pltpu.HBM),
+            pl.BlockSpec(memory_space=pltpu.HBM),
+            pl.BlockSpec(memory_space=pltpu.HBM),
+            pl.BlockSpec(memory_space=pltpu.HBM),
         ],
         out_specs=(
             pl.BlockSpec(memory_space=pl.ANY),
             pl.BlockSpec(memory_space=pltpu.VMEM),
         ),
         scratch_shapes=[
+            pltpu.VMEM((2, rows), jnp.int32),
+            pltpu.VMEM((coef,), f32),
             pltpu.VMEM((R, rows, Cs), bf16),
             pltpu.VMEM((B, R, refs, Cs), bf16),
             pltpu.VMEM((B, R, rows, width), f32),
@@ -462,21 +506,21 @@
             pltpu.VMEM((B, T, width, tile), bf16),
             pltpu.VMEM((B, T, width, tile), bf16),
             pltpu.VMEM((T, R, refs, tile), bf16),
-            dma((2,)),
+            dma((4,)),
             dma((R,)), dma((B, R)), dma((R,)), dma((R,)),
             dma((B, R)), dma((B, R)),
             dma((B, R)), dma((B, R)),
-            dma((R,)), dma((R,)),
+            dma((B, R)), dma((B, R)),
             dma((B, T)), dma((B, T)), dma((B, T)), dma((B, T)),
             dma((T, R)), dma((T, R)),
         ],
         compiler_params=pltpu.CompilerParams(
-            collective_id=0, has_side_effects=True, vmem_limit_bytes=50 * 1024 * 1024
+            collective_id=0, has_side_effects=True, vmem_limit_bytes=64 * 1024 * 1024 - 65536
         ),
         cost_estimate=pl.CostEstimate(
             flops=4 * R * rows * B * width * Cs, bytes_accessed=4 * rows * coef, transcendentals=0
         ),
-    )(images, routes, projections[0], noise_weights.reshape(R, 1, Cs))
+    )(images, routes.T, projections[0], noise_weights)
     return (sums.astype(f32)[None], norm[:, 0])
 
 

time: 112 us -> 92.6 us (0.83); the launches traced: 112 us -> 91.3 us
  Pallas kernels: 106 us -> 87.2 us
  local copies, waits for them, and re-layouts: 4.6 us -> 1.43 us
    pallas_call x1, Pallas kernels: 106 us -> 87.2 us  [split_coefficients(): pl.pallas_call(partial(kernel, R, B), out_shape=(jax.ShapeDtypeStruct((re...]
    unnamed x7 -> x0, local copies, waits for them, and re-layouts: 3.98 us -> none
where the time goes in v3:
time: 92.6 us; the launch traced here: 91.3 us
  Pallas kernels  87.2 us (94%)
  other arithmetic  2.08 us (2%)
  local copies, waits for them, and re-layouts  1.43 us (2%)
    pallas_call x1, Pallas kernels, split_coefficients(): pl.pallas_call(partial(kernel, R, B), out_shape=(jax.ShapeDtypeStruct((re...  87.2 us
    broadcast_in_dim x1, other arithmetic, split_coefficients(): return (sums.astype(f32)[None], norm[:, 0])  2.08 us

profile of v3, /device:TPU:20, one launch (start us, length us, event | category | flops | bytes accessed | tf_op | source)
XLA Modules:
  0.0 91.3 jit_solution(13959167891192634398)
XLA Ops:
  0.6 87.2 %shard_map.59 = (bf16[32,8192]{1,0:T(8,128)(2,1)}, f32[96,128]{1,0:T(8,128)}) custom-call(bf16[96,8192]{1,0:T(8,128)(2,1)} %images.1, s32[2,96]{1,0:T(2,128)} %bitcast.6, bf16[32,8192]{1,0:T(8,128)(2,1)} %bitcast.5, f32[8192]{0:T(1024)} %noise_in.1), custom_call_target="tpu_custom_call" | custom-call | flops 1610612736 | bytes 3145728 | tf_op jit(solution)/shard_map/pallas_call | solution.py:479
  87.8 1.4 %slice_reduce_fusion = f32[96]{0:T(128)} fusion(f32[96,128]{1,0:T(8,128)} %get-tuple-element.5), kind=kLoop, calls=%fused_computation.1 | loop fusion | bytes 768 | tf_op jit(solution)/shard_map/slice | solution.py:524
  89.3 2.1 %bitcast_convert_fusion = f32[1,32,8192]{2,1,0:T(8,128)} fusion(bf16[32,8192]{1,0:T(8,128)(2,1)} %get-tuple-element.4), kind=kLoop, calls=%fused_computation | loop fusion | flops 262144 | bytes 1572864 | tf_op jit(solution)/shard_map/broadcast_in_dim | solution.py:524

commit v4 on v3

--- a/solution.py
+++ b/solution.py
@@ -242,11 +242,11 @@
 
     send_own(r)
     own_image.start()
-    for k in masks:
-        image_copy(k).start()
     for k in order:
         arrived(PR.at[b, peers[k]], p_rcv.at[b, peers[k]])
         send_own(peers[k])
+    for k in masks:
+        image_copy(k).start()
 
     def score_chunk(src):
         scores = jnp.zeros((R * rows, width), jnp.float32)
@@ -345,10 +345,12 @@
     for c in range(1, B):
         spread = spread + jnp.exp(chunks[c] - highest)
     normalizer = highest + jnp.log(jnp.sum(spread, axis=1, keepdims=True))
-    for c in sorted(range(B), key=lambda c: min(c, B - 1 - c)):
+    for c in range(B):
         Q[c, r] = jnp.exp(chunks[c] - normalizer).astype(jnp.bfloat16)
+    lower = (2 * b < B).astype(jnp.int32)
+    for i in range(B):
         for k in masks:
-            post_copy(c, k).start()
+            post_copy(i + lower * (B - 1 - 2 * i), k).start()
     norm[...] = jnp.broadcast_to(normalizer, norm.shape)
     def product(d, t):
         cut = pl.ds(pl.multiple_of(t * tile, tile), tile)

time: 92.6 us -> 91.3 us (0.986); the launches traced: 91.3 us -> 91.1 us
  no operation moved by 1% of the time
where the time goes in v4:
time: 91.3 us; the launch traced here: 91.1 us
  Pallas kernels  86.9 us (95%)
  other arithmetic  2.08 us (2%)
  local copies, waits for them, and re-layouts  1.43 us (2%)
    pallas_call x1, Pallas kernels, split_coefficients(): pl.pallas_call(partial(kernel, R, B), out_shape=(jax.ShapeDtypeStruct((re...  86.9 us
    broadcast_in_dim x1, other arithmetic, split_coefficients(): return (sums.astype(f32)[None], norm[:, 0])  2.08 us

profile of v4, /device:TPU:20, one launch (start us, length us, event | category | flops | bytes accessed | tf_op | source)
XLA Modules:
  0.0 91.1 jit_solution(15215559879814534355)
XLA Ops:
  0.6 86.9 %shard_map.59 = (bf16[32,8192]{1,0:T(8,128)(2,1)}, f32[96,128]{1,0:T(8,128)}) custom-call(bf16[96,8192]{1,0:T(8,128)(2,1)} %images.1, s32[2,96]{1,0:T(2,128)} %bitcast.6, bf16[32,8192]{1,0:T(8,128)(2,1)} %bitcast.5, f32[8192]{0:T(1024)} %noise_in.1), custom_call_target="tpu_custom_call" | custom-call | flops 1610612736 | bytes 3145728 | tf_op jit(solution)/shard_map/pallas_call | solution.py:481
  87.6 1.4 %slice_reduce_fusion = f32[96]{0:T(128)} fusion(f32[96,128]{1,0:T(8,128)} %get-tuple-element.5), kind=kLoop, calls=%fused_computation.1 | loop fusion | bytes 768 | tf_op jit(solution)/shard_map/slice | solution.py:526
  89.0 2.1 %bitcast_convert_fusion = f32[1,32,8192]{2,1,0:T(8,128)} fusion(bf16[32,8192]{1,0:T(8,128)(2,1)} %get-tuple-element.4), kind=kLoop, calls=%fused_computation | loop fusion | flops 262144 | bytes 1572864 | tf_op jit(solution)/shard_map/broadcast_in_dim | solution.py:526
